TPU v7x, 512 devices: a whole 4x4x16 slice. The times are simulated.
512 devices in a mesh: kvseq: 64 (over y, z), tp: 8 (over x, core).
Axes of the slice: x: 4, y: 4, z: 16, core: 2. Of those that a mesh axis runs over, the one named last changes fastest.
Arguments:
- queries: bfloat16 [8, 16384], P(None, 'tp'), may hold values from -6 to 6
- incoming_keys: bfloat16 [8, 1024], P(None, 'tp'), may hold values from -6 to 6
- new_values: bfloat16 [8, 1024], P(None, 'tp'), may hold values from -6 to 6
- key_cache: bfloat16 [8, 4096, 8, 128], P(None, 'kvseq', 'tp'), may hold values from -6 to 6
- value_cache: bfloat16 [8, 4096, 8, 128], P(None, 'kvseq', 'tp'), may hold values from -6 to 6
- lengths: int32 [8], replicated, may hold values from 512 to 4096, as said below
- residual: bfloat16 [8, 16384], P(None, ('kvseq', 'tp')), may hold values from -1 to 1
- norm_gain: bfloat16 [16384], replicated, may hold values from 0.5 to 1.5
- o_weight: bfloat16 [8, 2048, 16384], P('tp', 'kvseq'), may hold values from -0.125 to 0.125
- gate_weight: bfloat16 [26624, 16384], P(('kvseq', 'tp')), may hold values from -0.046875 to 0.046875
- up_weight: bfloat16 [26624, 16384], P(('kvseq', 'tp')), may hold values from -0.046875 to 0.046875
Outputs:
- attended: bfloat16 [8, 8, 2048], P(None, 'tp', 'kvseq')
- updated: bfloat16 [8, 16384], P(None, ('kvseq', 'tp'))
- hidden: bfloat16 [8, 26624], P(None, ('kvseq', 'tp'))
Inputs may be any that keep to these rules, and one draw needn't show every extreme that they name: `lengths`: every row has at least 512 cached positions, and some row holds all 4096.
All inputs are finite; a program needn't handle non-finite values.
Results may differ from a plain program's by a relative error of at most 0.03.
Values may be sent and summed in bfloat16 or wider, within the bound.
A program may use at most 64 MiB of HBM per device.

v0:
```python
import math

import jax
import jax.numpy as jnp
from jax import lax
from jax.sharding import PartitionSpec as P

norm_eps = 1e-05


def body(
    queries,
    incoming_keys,
    new_values,
    key_cache,
    value_cache,
    lengths,
    residual,
    norm_gain,
    o_weight,
    gate_weight,
    up_weight,
):
    rows, span, heads_kv, head_dim = key_cache.shape
    group = queries.shape[1] // (heads_kv * head_dim)
    blocks = lax.axis_size("kvseq")
    block_id = lax.axis_index("kvseq")
    score_scale = 1.0 / math.sqrt(head_dim)
    query_head_count = queries.reshape(rows, heads_kv, group, head_dim)
    scores = (
        jnp.einsum(
            "bkgd,bskd->bkgs", query_head_count, key_cache, preferred_element_type=jnp.float32
        )
        * score_scale
    )
    posit = block_id * span + lax.broadcasted_iota(jnp.int32, (span,), 0)
    live = posit[None, None, None, :] < lengths[:, None, None, None]
    incoming_token = (
        jnp.einsum(
            "cuxt,cut->cux",
            query_head_count,
            incoming_keys.reshape(rows, heads_kv, head_dim),
            preferred_element_type=jnp.float32,
        )
        * score_scale
    )
    first = block_id == 0
    top = jnp.max(jnp.where(live, scores, -10000.0), axis=-1)
    top = jnp.where(first, jnp.maximum(top, incoming_token), top)
    probs = jnp.where(live, jnp.exp(scores - top[..., None]), 0.0)
    pnew = jnp.where(first, jnp.exp(incoming_token - top), 0.0)
    total = jnp.sum(probs, axis=-1) + pnew
    numer = jnp.einsum(
        "bkgs,bskd->bkgd",
        probs.astype(jnp.bfloat16),
        value_cache,
        preferred_element_type=jnp.float32,
    )
    pnew_low = lax.optimization_barrier(pnew.astype(jnp.bfloat16)).astype(jnp.float32)
    numer = numer + pnew_low[..., None] * new_values.reshape(rows, heads_kv, 1, head_dim).astype(
        jnp.float32
    )
    floor = jnp.maximum(total, 1.0)
    partial_value = (
        (numer / floor[..., None]).astype(jnp.bfloat16).reshape(rows, heads_kv * group * head_dim)
    )
    lse = (top + jnp.log(floor)).reshape(rows, heads_kv * group)
    width = partial_value.shape[1] // blocks
    per_head = max(width // head_dim, 1)
    head_start = block_id * width // head_dim
    peak = lax.pmax(lse, "kvseq")
    share = jnp.exp(lse - peak)
    weighted = (
        share[..., None]
        * partial_value.reshape(rows, heads_kv * group, head_dim).astype(jnp.float32)
    ).reshape(rows, -1)
    summed = lax.psum_scatter(weighted, "kvseq", scatter_dimension=1, tiled=True)
    totals = lax.psum(share, "kvseq")
    last = totals.ndim - 1
    mine = lax.dynamic_slice_in_dim(totals, head_start, per_head, last)
    attended = (summed / jnp.repeat(mine, width // per_head, axis=last)).astype(jnp.bfloat16)
    proj_weight = o_weight[0]
    cells = residual.shape[1]
    owner = lax.axis_index("kvseq") * lax.axis_size("tp") + lax.axis_index("tp")
    residual_rows = residual.astype(jnp.float32)
    contract = (((1,), (1,)), ((), ()))
    term = jnp.dot(attended, proj_weight, preferred_element_type=jnp.float32)
    own_cols = lax.dynamic_slice_in_dim(term, owner * cells, cells, 1) + residual_rows
    term = lax.dynamic_update_slice_in_dim(term, own_cols, owner * cells, 1)
    summed_all = lax.psum(term, ("kvseq", "tp"))
    inverse = lax.rsqrt(jnp.mean(summed_all * summed_all, axis=1, keepdims=True) + norm_eps)
    mine = lax.dynamic_slice_in_dim(summed_all, owner * cells, cells, 1)
    normed_all = (summed_all * inverse * norm_gain.astype(jnp.float32)[None, :]).astype(
        jnp.bfloat16
    )
    gate = lax.dot_general(normed_all, gate_weight, contract, preferred_element_type=jnp.float32)
    up = lax.dot_general(normed_all, up_weight, contract, preferred_element_type=jnp.float32)
    hidden = (jax.nn.silu(gate) * up).astype(jnp.bfloat16)
    return (attended.reshape(rows, 1, width), mine.astype(jnp.bfloat16), hidden)


def solution(mesh):
    in_specs = (
        P(None, "tp"),
        P(None, "tp"),
        P(None, "tp"),
        P(None, "kvseq", "tp", None),
        P(None, "kvseq", "tp", None),
        P(),
        P(None, ("kvseq", "tp")),
        P(),
        P("tp", "kvseq", None),
        P(("kvseq", "tp"), None),
        P(("kvseq", "tp"), None),
    )
    out_specs = (P(None, "tp", "kvseq"), P(None, ("kvseq", "tp")), P(None, ("kvseq", "tp")))
    return jax.shard_map(body, mesh=mesh, in_specs=in_specs, out_specs=out_specs, check_vma=False)
```

profile of v0, /device:TPU:1, one launch (start us, length us, event | category | flops | bytes accessed | tf_op | source)
XLA Modules:
  0.0 1318.5 jit_solution(17726034440325511114)
XLA Ops:
  7.2 0.0 reduce-scatter.4.cloned.1.call-start
  7.3 0.9 broadcast_compare_fusion
  8.2 0.9 fusion.15
  9.0 1.2 select_reduce_fusion
  10.3 0.2 fusion.10
  10.5 122.9 %pmax.7 = f32[8,16]{1,0:T(8,128)S(1)} all-reduce(f32[8,16]{1,0:T(8,128)S(1)} %get-tuple-element.3), channel_id=1, replica_groups=mesh['kvseq'=64,'tp'=8] {'kvseq'}, use_global_device_ids=true, to_apply=%region_2.3 | all-reduce | flops 128 | bytes 1024 | tf_op jit(solution)/shard_map/pmax | solution.py:71
  133.3 0.7 convert_element_type.45
  134.0 1.1 fusion.3
  135.2 1.3 copy.21
  136.5 0.0 all-reduce.2.cloned.1.call-start
  136.6 110.9 %psum.14 = f32[8,16]{1,0:T(8,128)S(1)} all-reduce(f32[8,16]{1,0:T(8,128)S(1)} %subtract_exponential_fusion), channel_id=1, replica_groups=mesh['kvseq'=64,'tp'=8] {'kvseq'}, use_global_device_ids=true, to_apply=%region_4.5 | all-reduce | flops 128 | bytes 1024 | tf_op jit(solution)/shard_map/psum | solution.py:78
  247.5 0.2 dynamic-slice_reduce_fusion
  247.7 585.5 %reduce-scatter.4.cloned.1.call-done = f32[32,8]{1,0:T(8,128)} async-done(((f32[2048,8]{1,0:T(8,128)}), f32[32,8]{1,0:T(8,128)}) %reduce-scatter.4.cloned.1.call-update) | async-done | bytes 1040
  833.2 0.8 copy.20
  833.9 0.3 fusion.5
  834.3 0.1 convert_add_fusion
  834.4 0.3 dynamic_update_slice.3
  834.6 0.8 copy-done.2
  835.5 0.7 fusion.24
  836.1 469.8 %all-reduce.2.cloned.1.call-done = f32[8,16384]{1,0:T(8,128)} async-done(((f32[8,16384]{1,0:T(8,128)}), f32[8,16384]{1,0:T(8,128)}) %all-reduce.2.cloned.1.call-update) | async-done | bytes 524304 | tf_op jit(solution)/shard_map/psum | solution.py:90
  1305.9 1.4 multiply_reduce_fusion
  1307.4 1.3 dynamic-slice_convert_fusion
  1308.7 1.7 fusion.20
  1310.4 1.2 fusion.4
  (22 shorter events, 0.1 us)
Async XLA Ops:
  7.2 1301.5 %copy-start = (bf16[52,16384]{1,0:T(8,128)(2,1)S(1)}, bf16[52,16384]{1,0:T(8,128)(2,1)}, u32[]{:S(2)}) copy-start(bf16[52,16384]{1,0:T(8,128)(2,1)} %param.20) | copy-start | bytes 5111812
  7.2 826.8 %copy-start.4 = (bf16[1,32,16384]{2,1,0:T(8,128)(2,1)S(1)}, bf16[1,32,16384]{2,1,0:T(8,128)(2,1)}, u32[]{:S(2)}) copy-start(bf16[1,32,16384]{2,1,0:T(8,128)(2,1)} %param.19) | copy-start | bytes 3145732
  7.2 826.0 %reduce-scatter.4.cloned.1.call-start = ((), (), s32[]{:S(2)}) async-start(), calls=%async_computation.2 | async-start | bytes 1064960
  135.2 699.1 %copy-start.6 = (bf16[8,32]{1,0:T(8,128)(2,1)S(1)}, bf16[8,32]{1,0:T(8,128)(2,1)}, u32[]{:S(2)}) copy-start(bf16[8,32]{1,0:T(8,128)(2,1)} %param.17) | copy-start | bytes 1540
  136.5 698.9 %copy-start.5 = (bf16[16384]{0:T(1024)(128)(2,1)S(1)}, bf16[16384]{0:T(1024)(128)(2,1)}, u32[]{:S(2)}) copy-start(bf16[16384]{0:T(1024)(128)(2,1)} %param.18) | copy-start | bytes 98308
  136.5 1169.4 %all-reduce.2.cloned.1.call-start = ((), (), s32[]{:S(2)}) async-start(), calls=%async_computation.1 | async-start | bytes 1048576 | tf_op jit(solution)/shard_map/psum | solution.py:90
  834.6 0.8 copy-start.2
  1305.9 4.5 copy-start.1
  1305.9 4.5 copy-start.3
Sparse Core Ops, SparseCore 0:
  136.7 696.4 reduce-scatter.3
  839.5 466.3 all-reduce.1
where the time goes:
time: 1320 us
  waiting for transfers between devices  1060 us (80%)
  blocking collectives  234 us (18%)
  between operations  14.2 us (1%)
    unnamed x3, waiting for transfers between devices  586 us
    psum x1, waiting for transfers between devices, body(): summed_all = lax.psum(term, ('kvseq', 'tp'))  470 us
    pmax x1, blocking collectives, body(): peak = lax.pmax(lse, 'kvseq')  123 us
    psum x1, blocking collectives, body(): totals = lax.psum(share, 'kvseq')  111 us
  transfers between devices with their start and end apart: 2, of which 2 were waited for; matrix products, arithmetic and copies ran while one was open for 0% of the time, Pallas kernels for 0%

commit v1 on v0

v1 whole, which is shorter than its diff:
```python
import math

import jax
import jax.numpy as jnp
from jax import lax
from jax.experimental import pallas as pl
from jax.experimental.pallas import tpu as pltpu
from jax.sharding import PartitionSpec as P

norm_eps = 1e-05
MESH = pl.DeviceIdType.MESH
F32, BF16 = jnp.float32, jnp.bfloat16
UNROLL = True


def place():
    kv, tp = lax.axis_index("kvseq"), lax.axis_index("tp")
    return kv // 16, kv % 16, tp // 2, tp % 2


def z_peer(k):
    y, z, x, c = place()
    step = jnp.where(k % 2 == 0, 8 + k // 2, 8 - (k + 1) // 2)
    return (y * 16 + (z + step) % 16, x * 2 + c)


def far_first(a):
    return jnp.where(a == 0, 2, jnp.where(a == 1, 1, jnp.where(a == 2, 3, 0)))


def plane_peer(k):
    y, z, x, c = place()
    py = (y + far_first(k // 8)) % 4
    px = (x + far_first((k // 2) % 4)) % 4
    return py, px, (c + 1 - k % 2) % 2


def loop(n, body):
    def step(k, carry):
        body(k)
        return carry

    lax.fori_loop(0, n, step, 0, unroll=UNROLL)


def kernel(
    lengths_ref,
    q_hbm,
    ik_hbm,
    nv_hbm,
    k_hbm,
    v_hbm,
    res_hbm,
    gain_hbm,
    ow_hbm,
    gate_hbm,
    up_hbm,
    att_out,
    upd_out,
    hid_out,
    q_ref,
    ik_ref,
    nv_ref,
    k_ref,
    v_ref,
    res_ref,
    gain_ref,
    ow,
    gate_w,
    up_w,
    gain32,
    s1,
    z1,
    rsrc,
    rbuf,
    psrc,
    pbuf,
    wbuf,
    z2src,
    z2,
    hsrc,
    hbuf,
    hg,
    local_sems,
    send_sems,
    recv_sems,
):
    y, z, x, c = place()
    t = x * 2 + c
    j = y * 16 + z
    slot_ty = t * 4 + y
    slot_m = y * 8 + t
    barrier = pltpu.get_barrier_semaphore()

    def greet_z(k):
        pl.semaphore_signal(barrier, inc=1, device_id=z_peer(k), device_id_type=MESH)

    def greet_plane(k):
        py, px, pc = plane_peer(k)
        pl.semaphore_signal(
            barrier, inc=1, device_id=(py * 16 + z, px * 2 + pc), device_id_type=MESH
        )

    loop(15, greet_z)
    loop(31, greet_plane)

    small = []
    for i, (src, dst) in enumerate(
        (
            (q_hbm, q_ref),
            (k_hbm, k_ref),
            (ik_hbm, ik_ref),
            (v_hbm, v_ref),
            (nv_hbm, nv_ref),
            (res_hbm, res_ref),
            (gain_hbm, gain_ref),
        )
    ):
        small.append(pltpu.make_async_copy(src, dst, local_sems.at[4 + i]))
        small[-1].start()
    ow_load = pltpu.make_async_copy(ow_hbm, ow, local_sems.at[0])
    gate_load = pltpu.make_async_copy(gate_hbm, gate_w, local_sems.at[1])
    up_load = pltpu.make_async_copy(up_hbm, up_w, local_sems.at[2])
    ow_load.start()
    gate_load.start()
    up_load.start()

    for i in range(5):
        small[i].wait()

    scale = 1.0 / math.sqrt(128)
    qs = [q_ref[:, 128 * h : 128 * h + 128].astype(F32) for h in range(16)]
    q_all = jnp.concatenate(qs, axis=0).astype(BF16)
    contract = (((1,), (1,)), ((), ()))
    s_all = lax.dot_general(q_all, k_ref[...], contract, preferred_element_type=F32) * scale
    row = lax.broadcasted_iota(jnp.int32, (8, 512), 0)
    lane = lax.broadcasted_iota(jnp.int32, (8, 512), 1)
    length = jnp.zeros((8, 512), jnp.int32)
    for b in range(8):
        length = jnp.where(row == b, lengths_ref[b], length)
    live = jnp.logical_and(lane // 64 == row, j * 64 + lane % 64 < length)
    ik = ik_ref[...].astype(F32)
    nv = nv_ref[...].astype(F32)
    first = j == 0
    probs, extra, floors, lses = [], [], [], []
    for h in range(16):
        s = s_all[8 * h : 8 * h + 8]
        fresh = jnp.sum(qs[h] * ik, axis=1, keepdims=True) * scale
        fresh = jnp.where(first, fresh, -1e30)
        top = jnp.max(jnp.where(live, s, -10000.0), axis=1, keepdims=True)
        top = jnp.maximum(top, fresh)
        p = jnp.where(live, jnp.exp(s - top), 0.0)
        pnew = jnp.exp(fresh - top)
        floor = jnp.maximum(jnp.sum(p, axis=1, keepdims=True) + pnew, 1.0)
        probs.append(p)
        extra.append(pnew.astype(BF16).astype(F32) * nv)
        floors.append(floor)
        lses.append(top + jnp.log(floor))
    p_all = jnp.concatenate(probs, axis=0).astype(BF16)
    numer = jnp.dot(p_all, v_ref[...], preferred_element_type=F32)
    part = [(numer[8 * h : 8 * h + 8] + extra[h]) / floors[h] for h in range(16)]

    block = lax.broadcasted_iota(jnp.int32, (8, 128), 1) // 32
    for zq in range(4):
        lse_tile = jnp.zeros((8, 128), F32)
        for yy in range(4):
            lse_tile = jnp.where(block == yy, lses[4 * yy + zq], lse_tile)
        for qq in range(4):
            tile = jnp.zeros((8, 128), F32)
            for yy in range(4):
                moved = part[4 * yy + zq]
                shift = (32 * (yy - qq)) % 128
                if shift:
                    moved = pltpu.roll(moved, shift, 1)
                tile = jnp.where(block == yy, moved, tile)
            s1[4 * zq + qq, 0:8, :] = tile
            s1[4 * zq + qq, 8:16, :] = lse_tile

    small[5].wait()
    small[6].wait()
    spot = lax.broadcasted_iota(jnp.int32, (32, 128), 1)
    want = lax.broadcasted_iota(jnp.int32, (32, 128), 0) + 32 * (t % 4)
    onehot = jnp.where(spot == want, 1.0, 0.0).astype(BF16)
    rtile = jnp.dot(res_ref[...], onehot, preferred_element_type=F32)
    rsrc[...] = rtile
    rbuf[t] = rtile
    gain32[...] = gain_ref[...].astype(F32)
    z1[z] = s1[z]

    pl.semaphore_wait(barrier, 46)

    def send_z1(k):
        kv, tp = z_peer(k)
        pltpu.make_async_remote_copy(
            src_ref=s1.at[kv % 16],
            dst_ref=z1.at[z],
            send_sem=send_sems.at[0],
            recv_sem=recv_sems.at[0],
            device_id=(kv, tp),
            device_id_type=MESH,
        ).start()

    loop(15, send_z1)

    ow_load.wait()

    def send_w(k):
        py, px, pc = plane_peer(k)
        column = pl.multiple_of(512 * (py * 8 + px * 2 + pc), 512)
        pltpu.make_async_remote_copy(
            src_ref=ow.at[:, pl.ds(column, 512)],
            dst_ref=wbuf.at[slot_ty],
            send_sem=send_sems.at[1],
            recv_sem=recv_sems.at[1],
            device_id=(py * 16 + z, px * 2 + pc),
            device_id_type=MESH,
        ).start()

    loop(31, send_w)
    own_column = pl.multiple_of(512 * slot_m, 512)
    own_w = pltpu.make_async_copy(
        ow.at[:, pl.ds(own_column, 512)], wbuf.at[slot_ty], local_sems.at[3]
    )
    own_w.start()

    def send_res(k):
        pltpu.make_async_remote_copy(
            src_ref=rsrc,
            dst_ref=rbuf.at[t],
            send_sem=send_sems.at[2],
            recv_sem=recv_sems.at[2],
            device_id=(j, (t + 1 + k) % 8),
            device_id_type=MESH,
        ).start()

    loop(7, send_res)

    def wait(ref, sem):
        pltpu.make_async_copy(ref, ref, sem).wait()

    wait(z1.at[pl.ds(0, 15)], recv_sems.at[0])
    tops = [z1[i, 8:16, :] for i in range(16)]
    peak = tops[0]
    for i in range(1, 16):
        peak = jnp.maximum(peak, tops[i])
    num = jnp.zeros((8, 128), F32)
    den = jnp.zeros((8, 128), F32)
    for i in range(16):
        w = jnp.exp(tops[i] - peak)
        num = num + w * z1[i, 0:8, :]
        den = den + w
    num = num / den
    den = peak + jnp.log(den)
    psrc[0:8, :] = num
    psrc[8:16, :] = den
    pbuf[slot_ty, 0:8, :] = num
    pbuf[slot_ty, 8:16, :] = den

    def send_p(k):
        py, px, pc = plane_peer(k)
        pltpu.make_async_remote_copy(
            src_ref=psrc,
            dst_ref=pbuf.at[slot_ty],
            send_sem=send_sems.at[3],
            recv_sem=recv_sems.at[3],
            device_id=(py * 16 + z, px * 2 + pc),
            device_id_type=MESH,
        ).start()

    loop(31, send_p)
    wait(pbuf.at[pl.ds(0, 31)], recv_sems.at[3])
    atts = []
    for tt in range(8):
        tops = [pbuf[4 * tt + i, 8:16, :] for i in range(4)]
        peak = jnp.maximum(jnp.maximum(tops[0], tops[1]), jnp.maximum(tops[2], tops[3]))
        num = jnp.zeros((8, 128), F32)
        den = jnp.zeros((8, 128), F32)
        for i in range(4):
            w = jnp.exp(tops[i] - peak)
            num = num + w * pbuf[4 * tt + i, 0:8, :]
            den = den + w
        atts.append(num / den)
    att = jnp.concatenate(atts, axis=1).astype(BF16)

    wait(wbuf.at[pl.ds(0, 31)], recv_sems.at[1])
    own_w.wait()
    h_part = jnp.dot(att, wbuf[...].reshape(1024, 512), preferred_element_type=F32)
    wait(rbuf.at[pl.ds(0, 7)], recv_sems.at[2])
    here = z // 2 == t
    r_low = jnp.where(here, rbuf[0] + rbuf[1] + rbuf[2] + rbuf[3], 0.0)
    r_high = jnp.where(here, rbuf[4] + rbuf[5] + rbuf[6] + rbuf[7], 0.0)
    r_both = jnp.concatenate([r_low, r_high], axis=1)
    h_even = h_part[:, 0:256] + jnp.where(z % 2 == 0, r_both, 0.0)
    h_odd = h_part[:, 256:512] + jnp.where(z % 2 == 1, r_both, 0.0)
    h_low = jnp.concatenate([h_even, h_odd], axis=0).astype(BF16)
    z2src[...] = h_low
    z2[z] = h_low

    def send_z2(k):
        kv, tp = z_peer(k)
        pltpu.make_async_remote_copy(
            src_ref=z2src,
            dst_ref=z2.at[z],
            send_sem=send_sems.at[4],
            recv_sem=recv_sems.at[4],
            device_id=(kv, tp),
            device_id_type=MESH,
        ).start()

    loop(15, send_z2)

    lane128 = lax.broadcasted_iota(jnp.int32, (128, 32), 0)
    col32 = lax.broadcasted_iota(jnp.int32, (128, 32), 1)
    mine = jnp.zeros((8, 128), F32)
    for tt in range(8):
        mine = jnp.where(t == tt, atts[tt], mine)
    pick = jnp.where(lane128 == col32 + 32 * y, 1.0, 0.0).astype(BF16)
    att_out[...] = jnp.dot(mine.astype(BF16), pick, preferred_element_type=F32).astype(BF16)

    wait(z2.at[pl.ds(0, 15)], recv_sems.at[4])
    h_sum = jnp.zeros((16, 256), F32)
    for i in range(16):
        h_sum = h_sum + z2[i].astype(F32)
    h_low = h_sum.astype(BF16)
    hsrc[...] = h_low
    hbuf[slot_m] = h_low

    def send_h(k):
        py, px, pc = plane_peer(k)
        pltpu.make_async_remote_copy(
            src_ref=hsrc,
            dst_ref=hbuf.at[slot_m],
            send_sem=send_sems.at[5],
            recv_sem=recv_sems.at[5],
            device_id=(py * 16 + z, px * 2 + pc),
            device_id_type=MESH,
        ).start()

    loop(31, send_h)
    gate_load.wait()
    up_load.wait()
    wait(hbuf.at[pl.ds(0, 31)], recv_sems.at[5])

    squares = jnp.zeros((8, 128), F32)
    gate = jnp.zeros((8, 52), F32)
    up = jnp.zeros((8, 52), F32)
    for m in range(32):
        full = hbuf[m].astype(F32)
        tiles = []
        for i in range(4):
            r, l = 8 * (i // 2), 128 * (i % 2)
            tile = full[r : r + 8, l : l + 128]
            squares = squares + tile * tile
            tiles.append(tile * gain32[4 * m + i : 4 * m + i + 1, :])
        hg[:, 512 * m : 512 * m + 512] = jnp.concatenate(tiles, axis=1).astype(BF16)
    for m in range(8):
        part_h = hg[:, 2048 * m : 2048 * m + 2048]
        gate = gate + lax.dot_general(
            part_h, gate_w[:, 2048 * m : 2048 * m + 2048], contract, preferred_element_type=F32
        )
        up = up + lax.dot_general(
            part_h, up_w[:, 2048 * m : 2048 * m + 2048], contract, preferred_element_type=F32
        )
    mean = jnp.sum(squares, axis=1, keepdims=True) * (1.0 / 16384)
    inverse = lax.rsqrt(mean + norm_eps)
    gate = gate * inverse
    up = up * inverse
    hid_out[...] = (gate / (1.0 + jnp.exp(-gate)) * up).astype(BF16)

    source = hbuf[y * 8 + z // 2].astype(F32)
    half = jnp.where(z % 2 == 0, source[0:8], source[8:16])
    tile = jnp.where(t // 4 == 0, half[:, 0:128], half[:, 128:256])
    pick = jnp.where(lane128 == col32 + 32 * (t % 4), 1.0, 0.0).astype(BF16)
    upd_out[...] = jnp.dot(tile.astype(BF16), pick, preferred_element_type=F32).astype(BF16)

    wait(s1.at[pl.ds(0, 15)], send_sems.at[0])
    wait(wbuf.at[pl.ds(0, 31)], send_sems.at[1])
    wait(rbuf.at[pl.ds(0, 7)], send_sems.at[2])
    wait(pbuf.at[pl.ds(0, 31)], send_sems.at[3])
    wait(z2.at[pl.ds(0, 15)], send_sems.at[4])
    wait(hbuf.at[pl.ds(0, 31)], send_sems.at[5])


def body(
    queries,
    incoming_keys,
    new_values,
    key_cache,
    value_cache,
    lengths,
    residual,
    norm_gain,
    o_weight,
    gate_weight,
    up_weight,
):
    vmem = pl.BlockSpec(memory_space=pltpu.VMEM)
    hbm = pl.BlockSpec(memory_space=pltpu.HBM)
    attended, updated, hidden = pl.pallas_call(
        kernel,
        out_shape=(
            jax.ShapeDtypeStruct((8, 32), BF16),
            jax.ShapeDtypeStruct((8, 32), BF16),
            jax.ShapeDtypeStruct((8, 52), BF16),
        ),
        in_specs=[pl.BlockSpec(memory_space=pltpu.SMEM)] + [hbm] * 10,
        out_specs=(vmem, vmem, vmem),
        scratch_shapes=[
            pltpu.VMEM((8, 2048), BF16),
            pltpu.VMEM((8, 128), BF16),
            pltpu.VMEM((8, 128), BF16),
            pltpu.VMEM((512, 128), BF16),
            pltpu.VMEM((512, 128), BF16),
            pltpu.VMEM((8, 32), BF16),
            pltpu.VMEM((128, 128), BF16),
            pltpu.VMEM((32, 16384), BF16),
            pltpu.VMEM((52, 16384), BF16),
            pltpu.VMEM((52, 16384), BF16),
            pltpu.VMEM((128, 128), F32),
            pltpu.VMEM((16, 16, 128), F32),
            pltpu.VMEM((16, 16, 128), F32),
            pltpu.VMEM((8, 128), F32),
            pltpu.VMEM((8, 8, 128), F32),
            pltpu.VMEM((16, 128), F32),
            pltpu.VMEM((32, 16, 128), F32),
            pltpu.VMEM((32, 32, 512), BF16),
            pltpu.VMEM((16, 256), BF16),
            pltpu.VMEM((16, 16, 256), BF16),
            pltpu.VMEM((16, 256), BF16),
            pltpu.VMEM((32, 16, 256), BF16),
            pltpu.VMEM((8, 16384), BF16),
            pltpu.SemaphoreType.DMA((11,)),
            pltpu.SemaphoreType.DMA((6,)),
            pltpu.SemaphoreType.DMA((6,)),
        ],
        compiler_params=pltpu.CompilerParams(
            collective_id=0, has_side_effects=True, vmem_limit_bytes=63 * 1024 * 1024
        ),
        name="decode_layer",
    )(
        lengths,
        queries,
        incoming_keys,
        new_values,
        key_cache.reshape(512, 128),
        value_cache.reshape(512, 128),
        residual,
        norm_gain.reshape(128, 128),
        o_weight.reshape(32, 16384),
        gate_weight,
        up_weight,
    )
    return attended.reshape(8, 1, 32), updated, hidden


def solution(mesh):
    in_specs = (
        P(None, "tp"),
        P(None, "tp"),
        P(None, "tp"),
        P(None, "kvseq", "tp", None),
        P(None, "kvseq", "tp", None),
        P(),
        P(None, ("kvseq", "tp")),
        P(),
        P("tp", "kvseq", None),
        P(("kvseq", "tp"), None),
        P(("kvseq", "tp"), None),
    )
    out_specs = (P(None, "tp", "kvseq"), P(None, ("kvseq", "tp")), P(None, ("kvseq", "tp")))
    return jax.shard_map(body, mesh=mesh, in_specs=in_specs, out_specs=out_specs, check_vma=False)
```

time: 1320 us -> 56.4 us (0.04)
  waiting for transfers between devices: 1060 us -> 0 us
  blocking collectives: 234 us -> 0 us
  Pallas kernels: 0 us -> 51.8 us
  between operations: 14.2 us -> 0.64 us
    unnamed x3 -> x0, waiting for transfers between devices: 586 us -> none
    psum x1 -> x0, waiting for transfers between devices: 470 us -> none  [body(): summed_all = lax.psum(term, ('kvseq', 'tp'))]
    pmax x1 -> x0, blocking collectives: 123 us -> none  [body(): peak = lax.pmax(lse, 'kvseq')]
    psum x1 -> x0, blocking collectives: 111 us -> none  [body(): totals = lax.psum(share, 'kvseq')]
    pallas_call x0 -> x1, Pallas kernels: none -> 51.8 us  [body(): pl.pallas_call(kernel, out_shape=(jax.ShapeDtypeStruct((8, 32), BF16), ja...]
  transfers between devices with their start and end apart: 2 -> 0, of which waited for: 2 -> 0; matrix products, arithmetic and copies ran while one was open for 0% -> 0% of each run, Pallas kernels for 0% -> 0%
where the time goes in v1:
time: 56.4 us; the launch traced here: 56.2 us
  Pallas kernels  51.8 us (92%)
  local copies, waits for them, and re-layouts  3.72 us (7%)
  between operations  0.64 us (1%)
    pallas_call x1, Pallas kernels, body(): pl.pallas_call(kernel, out_shape=(jax.ShapeDtypeStruct((8, 32), BF16), ja...  51.8 us
    unnamed x3, local copies, waits for them, and re-layouts  3.72 us

profile of v1, /device:TPU:1, one launch (start us, length us, event | category | flops | bytes accessed | tf_op | source)
XLA Modules:
  0.0 56.2 jit_solution(2202425348321353166)
XLA Ops:
  0.6 51.8 %decode_layer.1 = (bf16[8,32]{1,0:T(8,128)(2,1)}, bf16[8,32]{1,0:T(8,128)(2,1)}, bf16[8,52]{1,0:T(8,128)(2,1)}) custom-call(s32[8]{0:T(128)} %lengths_ref.1, bf16[8,2048]{1,0:T(8,128)(2,1)} %q_hbm.1, bf16[8,128]{1,0:T(8,128)(2,1)} %ik_hbm.1, bf16[8,128]{1,0:T(8,128)(2,1)} %nv_hbm.1, bf16[512,128]{1,0:T(8,128)(2,1)} %bitcast.6, bf16[512,128]{1,0:T(8,128)(2,1)} %bitcast.7, ...), custom_call_target="tpu_custom_call" | custom-call | tf_op jit(solution)/shard_map/decode_layer/pallas_call | solution.py:399
  52.4 1.2 %copy.17 = bf16[8,1,32]{2,0,1:T(8,128)(2,1)} copy(bf16[8,1,32]{2,0,1:T(8,128)(2,1)} %bitcast.9) | data formatting | bytes 1024
  53.7 1.2 %copy.18 = bf16[8,32]{1,0:T(8,128)(2,1)} copy(bf16[8,32]{1,0:T(8,128)(2,1)} %get-tuple-element.13) | data formatting | bytes 1024
  54.9 1.2 %copy.19 = bf16[8,52]{1,0:T(8,128)(2,1)} copy(bf16[8,52]{1,0:T(8,128)(2,1)} %get-tuple-element.14) | data formatting | bytes 1664

commit v2 on v1

--- a/solution.py
+++ b/solution.py
@@ -11,6 +11,7 @@
 MESH = pl.DeviceIdType.MESH
 F32, BF16 = jnp.float32, jnp.bfloat16
 UNROLL = True
+W_FIRST, W_SECOND = 12, 22
 
 
 def place():
@@ -21,6 +22,12 @@
 def z_peer(k):
     y, z, x, c = place()
     step = jnp.where(k % 2 == 0, 8 + k // 2, 8 - (k + 1) // 2)
+    return (y * 16 + (z + step) % 16, x * 2 + c)
+
+
+def z_near(k):
+    y, z, x, c = place()
+    step = jnp.where(k < 4, 4 - k, k + 8)
     return (y * 16 + (z + step) % 16, x * 2 + c)
 
 
@@ -35,12 +42,43 @@
     return py, px, (c + 1 - k % 2) % 2
 
 
-def loop(n, body):
+def loop(n, body, start=0):
     def step(k, carry):
         body(k)
         return carry
 
-    lax.fori_loop(0, n, step, 0, unroll=UNROLL)
+    lax.fori_loop(start, n, step, 0, unroll=UNROLL)
+
+
+def merge(nums, tops):
+    peak = tops[0]
+    for top in tops[1:]:
+        peak = jnp.maximum(peak, top)
+    num, den = 0.0, 0.0
+    for part, top in zip(nums, tops):
+        w = jnp.exp(top - peak)
+        num = num + w * part
+        den = den + w
+    return num / den, peak + jnp.log(den)
+
+
+def encode(num, top):
+    spot = lax.broadcasted_iota(jnp.int32, (8, 128), 1) % 32
+    high = top.astype(BF16).astype(F32)
+    middle = (top - high).astype(BF16).astype(F32)
+    low = top - high - middle
+    terms = jnp.where(spot == 0, high, jnp.where(spot == 1, middle, jnp.where(spot == 2, low, 0.0)))
+    return jnp.concatenate([num, terms], axis=0).astype(BF16)
+
+
+def decode(tiles):
+    n = tiles.shape[0]
+    a = lax.broadcasted_iota(jnp.int32, (128, 128), 0) // 32
+    b = lax.broadcasted_iota(jnp.int32, (128, 128), 1) // 32
+    ones = jnp.where(a == b, 1.0, 0.0).astype(BF16)
+    sums = jnp.dot(tiles.reshape(16 * n, 128), ones, preferred_element_type=F32)
+    values = tiles.astype(F32)
+    return [values[i, 0:8] for i in range(n)], [sums[16 * i + 8 : 16 * i + 16] for i in range(n)]
 
 
 def kernel(
@@ -70,7 +108,11 @@
     up_w,
     gain32,
     s1,
-    z1,
+    zd,
+    zp,
+    zm,
+    zrel,
+    zfin,
     rsrc,
     rbuf,
     psrc,
@@ -80,10 +122,13 @@
     z2,
     hsrc,
     hbuf,
-    hg,
+    att_v,
+    upd_v,
+    hid_v,
     local_sems,
     send_sems,
     recv_sems,
+    h_sems,
 ):
     y, z, x, c = place()
     t = x * 2 + c
@@ -93,7 +138,7 @@
     barrier = pltpu.get_barrier_semaphore()
 
     def greet_z(k):
-        pl.semaphore_signal(barrier, inc=1, device_id=z_peer(k), device_id_type=MESH)
+        pl.semaphore_signal(barrier, inc=1, device_id=z_near(k), device_id_type=MESH)
 
     def greet_plane(k):
         py, px, pc = plane_peer(k)
@@ -101,7 +146,7 @@
             barrier, inc=1, device_id=(py * 16 + z, px * 2 + pc), device_id_type=MESH
         )
 
-    loop(15, greet_z)
+    loop(8, greet_z)
     loop(31, greet_plane)
 
     small = []
@@ -173,8 +218,7 @@
                 if shift:
                     moved = pltpu.roll(moved, shift, 1)
                 tile = jnp.where(block == yy, moved, tile)
-            s1[4 * zq + qq, 0:8, :] = tile
-            s1[4 * zq + qq, 8:16, :] = lse_tile
+            s1[4 * zq + qq] = encode(tile, lse_tile)
 
     small[5].wait()
     small[6].wait()
@@ -184,23 +228,30 @@
     rtile = jnp.dot(res_ref[...], onehot, preferred_element_type=F32)
     rsrc[...] = rtile
     rbuf[t] = rtile
-    gain32[...] = gain_ref[...].astype(F32)
-    z1[z] = s1[z]
-
-    pl.semaphore_wait(barrier, 46)
-
-    def send_z1(k):
-        kv, tp = z_peer(k)
+    gain32[...] = gain_ref[...].astype(F32).reshape(4, 32, 128)
+    zd[3] = s1[z]
+    zp[4] = s1[(z + 4) % 16]
+    zm[3] = s1[(z + 12) % 16]
+
+    pl.semaphore_wait(barrier, 39)
+
+    def send_z1(src, dst, step, sem):
         pltpu.make_async_remote_copy(
-            src_ref=s1.at[kv % 16],
-            dst_ref=z1.at[z],
-            send_sem=send_sems.at[0],
-            recv_sem=recv_sems.at[0],
-            device_id=(kv, tp),
+            src_ref=src,
+            dst_ref=dst,
+            send_sem=send_sems.at[sem],
+            recv_sem=recv_sems.at[sem],
+            device_id=(y * 16 + (z + step) % 16, t),
             device_id_type=MESH,
         ).start()
 
-    loop(15, send_z1)
+    for d in (4, 3, 2, 1):
+        send_z1(s1.at[(z + d + 4) % 16], zp.at[d - 1], d, 0)
+        if d < 4:
+            send_z1(s1.at[(z + 12 - d) % 16], zm.at[d - 1], 16 - d, 6)
+    for d in (3, 2, 1):
+        send_z1(s1.at[(z + d) % 16], zd.at[3 + d], d, 7)
+        send_z1(s1.at[(z + 16 - d) % 16], zd.at[3 - d], 16 - d, 7)
 
     ow_load.wait()
 
@@ -216,7 +267,7 @@
             device_id_type=MESH,
         ).start()
 
-    loop(31, send_w)
+    loop(W_FIRST, send_w)
     own_column = pl.multiple_of(512 * slot_m, 512)
     own_w = pltpu.make_async_copy(
         ow.at[:, pl.ds(own_column, 512)], wbuf.at[slot_ty], local_sems.at[3]
@@ -238,23 +289,20 @@
     def wait(ref, sem):
         pltpu.make_async_copy(ref, ref, sem).wait()
 
-    wait(z1.at[pl.ds(0, 15)], recv_sems.at[0])
-    tops = [z1[i, 8:16, :] for i in range(16)]
-    peak = tops[0]
-    for i in range(1, 16):
-        peak = jnp.maximum(peak, tops[i])
-    num = jnp.zeros((8, 128), F32)
-    den = jnp.zeros((8, 128), F32)
-    for i in range(16):
-        w = jnp.exp(tops[i] - peak)
-        num = num + w * z1[i, 0:8, :]
-        den = den + w
-    num = num / den
-    den = peak + jnp.log(den)
-    psrc[0:8, :] = num
-    psrc[8:16, :] = den
-    pbuf[slot_ty, 0:8, :] = num
-    pbuf[slot_ty, 8:16, :] = den
+    wait(zp.at[pl.ds(0, 4)], recv_sems.at[0])
+    zrel[0] = encode(*merge(*decode(zp[...])))
+    send_z1(zrel.at[0], zfin.at[0], 4, 8)
+    wait(zm.at[pl.ds(0, 3)], recv_sems.at[6])
+    zrel[1] = encode(*merge(*decode(zm[...])))
+    send_z1(zrel.at[1], zfin.at[1], 12, 8)
+    loop(W_SECOND, send_w, W_FIRST)
+    wait(zd.at[pl.ds(0, 6)], recv_sems.at[7])
+    num, top = merge(*decode(zd[...]))
+    wait(zfin, recv_sems.at[8])
+    nums, tops = decode(zfin[...])
+    tile = encode(*merge([num] + nums, [top] + tops))
+    psrc[...] = tile
+    pbuf[slot_ty] = tile
 
     def send_p(k):
         py, px, pc = plane_peer(k)
@@ -268,18 +316,12 @@
         ).start()
 
     loop(31, send_p)
+    loop(31, send_w, W_SECOND)
     wait(pbuf.at[pl.ds(0, 31)], recv_sems.at[3])
-    atts = []
-    for tt in range(8):
-        tops = [pbuf[4 * tt + i, 8:16, :] for i in range(4)]
-        peak = jnp.maximum(jnp.maximum(tops[0], tops[1]), jnp.maximum(tops[2], tops[3]))
-        num = jnp.zeros((8, 128), F32)
-        den = jnp.zeros((8, 128), F32)
-        for i in range(4):
-            w = jnp.exp(tops[i] - peak)
-            num = num + w * pbuf[4 * tt + i, 0:8, :]
-            den = den + w
-        atts.append(num / den)
+    nums, tops = decode(pbuf[...])
+    atts = [
+        merge(nums[4 * i : 4 * i + 4], tops[4 * i : 4 * i + 4])[0] for i in range(8)
+    ]
     att = jnp.concatenate(atts, axis=1).astype(BF16)
 
     wait(wbuf.at[pl.ds(0, 31)], recv_sems.at[1])
@@ -315,7 +357,10 @@
     for tt in range(8):
         mine = jnp.where(t == tt, atts[tt], mine)
     pick = jnp.where(lane128 == col32 + 32 * y, 1.0, 0.0).astype(BF16)
-    att_out[...] = jnp.dot(mine.astype(BF16), pick, preferred_element_type=F32).astype(BF16)
+    att_v[...] = jnp.dot(mine.astype(BF16), pick, preferred_element_type=F32).astype(BF16)
+
+    att_save = pltpu.make_async_copy(att_v, att_out, local_sems.at[11])
+    att_save.start()
 
     wait(z2.at[pl.ds(0, 15)], recv_sems.at[4])
     h_sum = jnp.zeros((16, 256), F32)
@@ -331,7 +376,7 @@
             src_ref=hsrc,
             dst_ref=hbuf.at[slot_m],
             send_sem=send_sems.at[5],
-            recv_sem=recv_sems.at[5],
+            recv_sem=h_sems.at[k // 8],
             device_id=(py * 16 + z, px * 2 + pc),
             device_id_type=MESH,
         ).start()
@@ -339,46 +384,66 @@
     loop(31, send_h)
     gate_load.wait()
     up_load.wait()
-    wait(hbuf.at[pl.ds(0, 31)], recv_sems.at[5])
-
     squares = jnp.zeros((8, 128), F32)
     gate = jnp.zeros((8, 52), F32)
     up = jnp.zeros((8, 52), F32)
-    for m in range(32):
-        full = hbuf[m].astype(F32)
+    for g, step in enumerate((2, 1, 3, 0)):
+        from_y = (y + 4 - step) % 4
+        wait(hbuf.at[pl.ds(0, 8 if step else 7)], h_sems.at[g])
+        gains = gain32[from_y]
         tiles = []
-        for i in range(4):
-            r, l = 8 * (i // 2), 128 * (i % 2)
-            tile = full[r : r + 8, l : l + 128]
-            squares = squares + tile * tile
-            tiles.append(tile * gain32[4 * m + i : 4 * m + i + 1, :])
-        hg[:, 512 * m : 512 * m + 512] = jnp.concatenate(tiles, axis=1).astype(BF16)
-    for m in range(8):
-        part_h = hg[:, 2048 * m : 2048 * m + 2048]
+        for m in range(8):
+            full = hbuf[8 * from_y + m].astype(F32)
+            for i in range(4):
+                r, l = 8 * (i // 2), 128 * (i % 2)
+                tile = full[r : r + 8, l : l + 128]
+                squares = squares + tile * tile
+                tiles.append(tile * gains[4 * m + i : 4 * m + i + 1, :])
+        part_h = jnp.concatenate(tiles, axis=1).astype(BF16)
+        columns = pl.ds(pl.multiple_of(4096 * from_y, 4096), 4096)
         gate = gate + lax.dot_general(
-            part_h, gate_w[:, 2048 * m : 2048 * m + 2048], contract, preferred_element_type=F32
+            part_h, gate_w[:, columns], contract, preferred_element_type=F32
         )
-        up = up + lax.dot_general(
-            part_h, up_w[:, 2048 * m : 2048 * m + 2048], contract, preferred_element_type=F32
-        )
+        up = up + lax.dot_general(part_h, up_w[:, columns], contract, preferred_element_type=F32)
     mean = jnp.sum(squares, axis=1, keepdims=True) * (1.0 / 16384)
     inverse = lax.rsqrt(mean + norm_eps)
     gate = gate * inverse
     up = up * inverse
-    hid_out[...] = (gate / (1.0 + jnp.exp(-gate)) * up).astype(BF16)
+    hid_v[...] = (gate / (1.0 + jnp.exp(-gate)) * up).astype(BF16)
+    hid_save = pltpu.make_async_copy(hid_v, hid_out, local_sems.at[12])
+    hid_save.start()
 
     source = hbuf[y * 8 + z // 2].astype(F32)
     half = jnp.where(z % 2 == 0, source[0:8], source[8:16])
     tile = jnp.where(t // 4 == 0, half[:, 0:128], half[:, 128:256])
     pick = jnp.where(lane128 == col32 + 32 * (t % 4), 1.0, 0.0).astype(BF16)
-    upd_out[...] = jnp.dot(tile.astype(BF16), pick, preferred_element_type=F32).astype(BF16)
-
-    wait(s1.at[pl.ds(0, 15)], send_sems.at[0])
+    upd_v[...] = jnp.dot(tile.astype(BF16), pick, preferred_element_type=F32).astype(BF16)
+    upd_save = pltpu.make_async_copy(upd_v, upd_out, local_sems.at[13])
+    upd_save.start()
+
+    wait(zp.at[pl.ds(0, 4)], send_sems.at[0])
+    wait(zm.at[pl.ds(0, 3)], send_sems.at[6])
+    wait(zd.at[pl.ds(0, 6)], send_sems.at[7])
+    wait(zfin, send_sems.at[8])
     wait(wbuf.at[pl.ds(0, 31)], send_sems.at[1])
     wait(rbuf.at[pl.ds(0, 7)], send_sems.at[2])
     wait(pbuf.at[pl.ds(0, 31)], send_sems.at[3])
     wait(z2.at[pl.ds(0, 15)], send_sems.at[4])
     wait(hbuf.at[pl.ds(0, 31)], send_sems.at[5])
+    att_save.wait()
+    upd_save.wait()
+    hid_save.wait()
+
+
+def save(a, b, c, a_out, b_out, c_out, sems):
+    copies = [
+        pltpu.make_async_copy(src, dst, sems.at[i])
+        for i, (src, dst) in enumerate(((a, a_out), (b, b_out), (c, c_out)))
+    ]
+    for copy in copies:
+        copy.start()
+    for copy in copies:
+        copy.wait()
 
 
 def body(
@@ -394,7 +459,6 @@
     gate_weight,
     up_weight,
 ):
-    vmem = pl.BlockSpec(memory_space=pltpu.VMEM)
     hbm = pl.BlockSpec(memory_space=pltpu.HBM)
     attended, updated, hidden = pl.pallas_call(
         kernel,
@@ -404,7 +468,7 @@
             jax.ShapeDtypeStruct((8, 52), BF16),
         ),
         in_specs=[pl.BlockSpec(memory_space=pltpu.SMEM)] + [hbm] * 10,
-        out_specs=(vmem, vmem, vmem),
+        out_specs=(hbm, hbm, hbm),
         scratch_shapes=[
             pltpu.VMEM((8, 2048), BF16),
             pltpu.VMEM((8, 128), BF16),
@@ -416,22 +480,29 @@
             pltpu.VMEM((32, 16384), BF16),
             pltpu.VMEM((52, 16384), BF16),
             pltpu.VMEM((52, 16384), BF16),
-            pltpu.VMEM((128, 128), F32),
-            pltpu.VMEM((16, 16, 128), F32),
-            pltpu.VMEM((16, 16, 128), F32),
+            pltpu.VMEM((4, 32, 128), F32),
+            pltpu.VMEM((16, 16, 128), BF16),
+            pltpu.VMEM((7, 16, 128), BF16),
+            pltpu.VMEM((5, 16, 128), BF16),
+            pltpu.VMEM((4, 16, 128), BF16),
+            pltpu.VMEM((2, 16, 128), BF16),
+            pltpu.VMEM((2, 16, 128), BF16),
             pltpu.VMEM((8, 128), F32),
             pltpu.VMEM((8, 8, 128), F32),
-            pltpu.VMEM((16, 128), F32),
-            pltpu.VMEM((32, 16, 128), F32),
+            pltpu.VMEM((16, 128), BF16),
+            pltpu.VMEM((32, 16, 128), BF16),
             pltpu.VMEM((32, 32, 512), BF16),
             pltpu.VMEM((16, 256), BF16),
             pltpu.VMEM((16, 16, 256), BF16),
             pltpu.VMEM((16, 256), BF16),
             pltpu.VMEM((32, 16, 256), BF16),
-            pltpu.VMEM((8, 16384), BF16),
-            pltpu.SemaphoreType.DMA((11,)),
-            pltpu.SemaphoreType.DMA((6,)),
-            pltpu.SemaphoreType.DMA((6,)),
+            pltpu.VMEM((8, 32), BF16),
+            pltpu.VMEM((8, 32), BF16),
+            pltpu.VMEM((8, 52), BF16),
+            pltpu.SemaphoreType.DMA((14,)),
+            pltpu.SemaphoreType.DMA((9,)),
+            pltpu.SemaphoreType.DMA((9,)),
+            pltpu.SemaphoreType.DMA((4,)),
         ],
         compiler_params=pltpu.CompilerParams(
             collective_id=0, has_side_effects=True, vmem_limit_bytes=63 * 1024 * 1024
@@ -450,6 +521,15 @@
         gate_weight,
         up_weight,
     )
+    attended, updated, hidden = pl.pallas_call(
+        save,
+        out_shape=tuple(jax.ShapeDtypeStruct(a.shape, a.dtype) for a in (attended, updated, hidden)),
+        in_specs=[hbm] * 3,
+        out_specs=(hbm, hbm, hbm),
+        scratch_shapes=[pltpu.SemaphoreType.DMA((3,))],
+        compiler_params=pltpu.CompilerParams(vmem_limit_bytes=63 * 1024 * 1024),
+        name="save_results",
+    )(attended, updated, hidden)
     return attended.reshape(8, 1, 32), updated, hidden
 
 

time: 56.4 us -> 51.7 us (0.917)
  local copies, waits for them, and re-layouts: 3.72 us -> 0 us
  Pallas kernels: 51.8 us -> 50.9 us
    unnamed x3 -> x0, local copies, waits for them, and re-layouts: 3.72 us -> none
    pallas_call x1, Pallas kernels: 51.8 us -> 49.6 us  [body(): pl.pallas_call(kernel, out_shape=(jax.ShapeDtypeStruct((8, 32), BF16), ja...]
    pallas_call x0 -> x1, Pallas kernels: none -> 1.32 us  [body(): pl.pallas_call(save, out_shape=tuple((jax.ShapeDtypeStruct(a.shape, a.dty...]
where the time goes in v2:
time: 51.7 us; the launch traced here: 51.6 us
  Pallas kernels  50.9 us (98%)
  between operations  0.64 us (1%)
    pallas_call x1, Pallas kernels, body(): pl.pallas_call(kernel, out_shape=(jax.ShapeDtypeStruct((8, 32), BF16), ja...  49.6 us
    pallas_call x1, Pallas kernels, body(): pl.pallas_call(save, out_shape=tuple((jax.ShapeDtypeStruct(a.shape, a.dty...  1.32 us

profile of v2, /device:TPU:1, one launch (start us, length us, event | category | flops | bytes accessed | tf_op | source)
XLA Modules:
  0.0 51.6 jit_solution(3705443256757922514)
XLA Ops:
  0.6 49.6 %decode_layer.1 = (bf16[8,32]{1,0:T(8,128)(2,1)}, bf16[8,32]{1,0:T(8,128)(2,1)}, bf16[8,52]{1,0:T(8,128)(2,1)}) custom-call(s32[8]{0:T(128)} %lengths_ref.1, bf16[8,2048]{1,0:T(8,128)(2,1)} %q_hbm.1, bf16[8,128]{1,0:T(8,128)(2,1)} %ik_hbm.1, bf16[8,128]{1,0:T(8,128)(2,1)} %nv_hbm.1, bf16[512,128]{1,0:T(8,128)(2,1)} %bitcast.6, bf16[512,128]{1,0:T(8,128)(2,1)} %bitcast.7, ...), custom_call_target="tpu_custom_call" | custom-call | tf_op jit(solution)/shard_map/decode_layer/pallas_call | solution.py:463
  50.3 1.3 %save_results.1 = (bf16[8,32]{1,0:T(8,128)(2,1)}, bf16[8,32]{1,0:T(8,128)(2,1)}, bf16[8,52]{1,0:T(8,128)(2,1)}) custom-call(bf16[8,32]{1,0:T(8,128)(2,1)} %get-tuple-element.9.a, bf16[8,32]{1,0:T(8,128)(2,1)} %get-tuple-element.10.b, bf16[8,52]{1,0:T(8,128)(2,1)} %get-tuple-element.11.c), custom_call_target="tpu_custom_call" | custom-call | tf_op jit(solution)/shard_map/save_results/pallas_call | solution.py:524

commit v3 on v2

--- a/solution.py
+++ b/solution.py
@@ -27,7 +27,7 @@
 
 def z_near(k):
     y, z, x, c = place()
-    step = jnp.where(k < 4, 4 - k, k + 8)
+    step = jnp.where(k % 2 == 0, 4 - k // 2, 12 + k // 2)
     return (y * 16 + (z + step) % 16, x * 2 + c)
 
 
@@ -40,6 +40,13 @@
     py = (y + far_first(k // 8)) % 4
     px = (x + far_first((k // 2) % 4)) % 4
     return py, px, (c + 1 - k % 2) % 2
+
+
+def core_first(k):
+    y, z, x, c = place()
+    other = k >= 15
+    i = jnp.where(other, k - 15, k)
+    return (y + far_first(i // 4)) % 4, (x + far_first(i % 4)) % 4, jnp.where(other, 1 - c, c)
 
 
 def loop(n, body, start=0):
@@ -129,6 +136,7 @@
     send_sems,
     recv_sems,
     h_sems,
+    ready,
 ):
     y, z, x, c = place()
     t = x * 2 + c
@@ -141,13 +149,10 @@
         pl.semaphore_signal(barrier, inc=1, device_id=z_near(k), device_id_type=MESH)
 
     def greet_plane(k):
-        py, px, pc = plane_peer(k)
+        py, px, pc = core_first(k)
         pl.semaphore_signal(
             barrier, inc=1, device_id=(py * 16 + z, px * 2 + pc), device_id_type=MESH
         )
-
-    loop(8, greet_z)
-    loop(31, greet_plane)
 
     small = []
     for i, (src, dst) in enumerate(
@@ -162,7 +167,14 @@
         )
     ):
         small.append(pltpu.make_async_copy(src, dst, local_sems.at[4 + i]))
-        small[-1].start()
+        if i < 5:
+            small[-1].start()
+    loop(8, greet_z)
+    loop(15, greet_plane)
+    partner = (j, x * 2 + 1 - c)
+    pl.semaphore_signal(barrier, inc=1, device_id=partner, device_id_type=MESH)
+    small[5].start()
+    small[6].start()
     ow_load = pltpu.make_async_copy(ow_hbm, ow, local_sems.at[0])
     gate_load = pltpu.make_async_copy(gate_hbm, gate_w, local_sems.at[1])
     up_load = pltpu.make_async_copy(up_hbm, up_w, local_sems.at[2])
@@ -233,7 +245,8 @@
     zp[4] = s1[(z + 4) % 16]
     zm[3] = s1[(z + 12) % 16]
 
-    pl.semaphore_wait(barrier, 39)
+    pl.semaphore_wait(barrier, 24)
+    pl.semaphore_signal(ready, inc=1, device_id=partner, device_id_type=MESH)
 
     def send_z1(src, dst, step, sem):
         pltpu.make_async_remote_copy(
@@ -256,7 +269,7 @@
     ow_load.wait()
 
     def send_w(k):
-        py, px, pc = plane_peer(k)
+        py, px, pc = core_first(k)
         column = pl.multiple_of(512 * (py * 8 + px * 2 + pc), 512)
         pltpu.make_async_remote_copy(
             src_ref=ow.at[:, pl.ds(column, 512)],
@@ -284,6 +297,7 @@
             device_id_type=MESH,
         ).start()
 
+    pl.semaphore_wait(ready, 1)
     loop(7, send_res)
 
     def wait(ref, sem):
@@ -405,6 +419,14 @@
             part_h, gate_w[:, columns], contract, preferred_element_type=F32
         )
         up = up + lax.dot_general(part_h, up_w[:, columns], contract, preferred_element_type=F32)
+    source = hbuf[y * 8 + z // 2].astype(F32)
+    half = jnp.where(z % 2 == 0, source[0:8], source[8:16])
+    tile = jnp.where(t // 4 == 0, half[:, 0:128], half[:, 128:256])
+    pick = jnp.where(lane128 == col32 + 32 * (t % 4), 1.0, 0.0).astype(BF16)
+    upd_v[...] = jnp.dot(tile.astype(BF16), pick, preferred_element_type=F32).astype(BF16)
+    upd_save = pltpu.make_async_copy(upd_v, upd_out, local_sems.at[13])
+    upd_save.start()
+
     mean = jnp.sum(squares, axis=1, keepdims=True) * (1.0 / 16384)
     inverse = lax.rsqrt(mean + norm_eps)
     gate = gate * inverse
@@ -412,14 +434,6 @@
     hid_v[...] = (gate / (1.0 + jnp.exp(-gate)) * up).astype(BF16)
     hid_save = pltpu.make_async_copy(hid_v, hid_out, local_sems.at[12])
     hid_save.start()
-
-    source = hbuf[y * 8 + z // 2].astype(F32)
-    half = jnp.where(z % 2 == 0, source[0:8], source[8:16])
-    tile = jnp.where(t // 4 == 0, half[:, 0:128], half[:, 128:256])
-    pick = jnp.where(lane128 == col32 + 32 * (t % 4), 1.0, 0.0).astype(BF16)
-    upd_v[...] = jnp.dot(tile.astype(BF16), pick, preferred_element_type=F32).astype(BF16)
-    upd_save = pltpu.make_async_copy(upd_v, upd_out, local_sems.at[13])
-    upd_save.start()
 
     wait(zp.at[pl.ds(0, 4)], send_sems.at[0])
     wait(zm.at[pl.ds(0, 3)], send_sems.at[6])
@@ -503,6 +517,7 @@
             pltpu.SemaphoreType.DMA((9,)),
             pltpu.SemaphoreType.DMA((9,)),
             pltpu.SemaphoreType.DMA((4,)),
+            pltpu.SemaphoreType.REGULAR,
         ],
         compiler_params=pltpu.CompilerParams(
             collective_id=0, has_side_effects=True, vmem_limit_bytes=63 * 1024 * 1024

time: 51.7 us -> 50.3 us (0.973)
  Pallas kernels: 50.9 us -> 49.5 us
    pallas_call x1, Pallas kernels: 49.6 us -> 48.2 us  [body(): pl.pallas_call(kernel, out_shape=(jax.ShapeDtypeStruct((8, 32), BF16), ja...]
where the time goes in v3:
time: 50.3 us; the launch traced here: 50.2 us
  Pallas kernels  49.5 us (98%)
  between operations  0.64 us (1%)
    pallas_call x1, Pallas kernels, body(): pl.pallas_call(kernel, out_shape=(jax.ShapeDtypeStruct((8, 32), BF16), ja...  48.2 us
    pallas_call x1, Pallas kernels, body(): pl.pallas_call(save, out_shape=tuple((jax.ShapeDtypeStruct(a.shape, a.dty...  1.32 us

profile of v3, /device:TPU:1, one launch (start us, length us, event | category | flops | bytes accessed | tf_op | source)
XLA Modules:
  0.0 50.2 jit_solution(1264386448996682156)
XLA Ops:
  0.6 48.2 %decode_layer.1 = (bf16[8,32]{1,0:T(8,128)(2,1)}, bf16[8,32]{1,0:T(8,128)(2,1)}, bf16[8,52]{1,0:T(8,128)(2,1)}) custom-call(s32[8]{0:T(128)} %lengths_ref.1, bf16[8,2048]{1,0:T(8,128)(2,1)} %q_hbm.1, bf16[8,128]{1,0:T(8,128)(2,1)} %ik_hbm.1, bf16[8,128]{1,0:T(8,128)(2,1)} %nv_hbm.1, bf16[512,128]{1,0:T(8,128)(2,1)} %bitcast.6, bf16[512,128]{1,0:T(8,128)(2,1)} %bitcast.7, ...), custom_call_target="tpu_custom_call" | custom-call | tf_op jit(solution)/shard_map/decode_layer/pallas_call | solution.py:477
  48.8 1.3 %save_results.1 = (bf16[8,32]{1,0:T(8,128)(2,1)}, bf16[8,32]{1,0:T(8,128)(2,1)}, bf16[8,52]{1,0:T(8,128)(2,1)}) custom-call(bf16[8,32]{1,0:T(8,128)(2,1)} %get-tuple-element.9.a, bf16[8,32]{1,0:T(8,128)(2,1)} %get-tuple-element.10.b, bf16[8,52]{1,0:T(8,128)(2,1)} %get-tuple-element.11.c), custom_call_target="tpu_custom_call" | custom-call | tf_op jit(solution)/shard_map/save_results/pallas_call | solution.py:539

commit v4 on v3

--- a/solution.py
+++ b/solution.py
@@ -401,7 +401,7 @@
     squares = jnp.zeros((8, 128), F32)
     gate = jnp.zeros((8, 52), F32)
     up = jnp.zeros((8, 52), F32)
-    for g, step in enumerate((2, 1, 3, 0)):
+    for g, step in ((3, 0), (2, 3), (1, 1), (0, 2)):
         from_y = (y + 4 - step) % 4
         wait(hbuf.at[pl.ds(0, 8 if step else 7)], h_sems.at[g])
         gains = gain32[from_y]

time: 50.3 us -> 49.7 us (0.988)
    pallas_call x1, Pallas kernels: 48.2 us -> 47.6 us  [body(): pl.pallas_call(kernel, out_shape=(jax.ShapeDtypeStruct((8, 32), BF16), ja...]
where the time goes in v4:
time: 49.7 us; the launch traced here: 49.6 us
  Pallas kernels  49 us (99%)
  between operations  0.64 us (1%)
    pallas_call x1, Pallas kernels, body(): pl.pallas_call(kernel, out_shape=(jax.ShapeDtypeStruct((8, 32), BF16), ja...  47.6 us
    pallas_call x1, Pallas kernels, body(): pl.pallas_call(save, out_shape=tuple((jax.ShapeDtypeStruct(a.shape, a.dty...  1.32 us

profile of v4, /device:TPU:1, one launch (start us, length us, event | category | flops | bytes accessed | tf_op | source)
XLA Modules:
  0.0 49.6 jit_solution(369881686219929714)
XLA Ops:
  0.6 47.6 %decode_layer.1 = (bf16[8,32]{1,0:T(8,128)(2,1)}, bf16[8,32]{1,0:T(8,128)(2,1)}, bf16[8,52]{1,0:T(8,128)(2,1)}) custom-call(s32[8]{0:T(128)} %lengths_ref.1, bf16[8,2048]{1,0:T(8,128)(2,1)} %q_hbm.1, bf16[8,128]{1,0:T(8,128)(2,1)} %ik_hbm.1, bf16[8,128]{1,0:T(8,128)(2,1)} %nv_hbm.1, bf16[512,128]{1,0:T(8,128)(2,1)} %bitcast.6, bf16[512,128]{1,0:T(8,128)(2,1)} %bitcast.7, ...), custom_call_target="tpu_custom_call" | custom-call | tf_op jit(solution)/shard_map/decode_layer/pallas_call | solution.py:477
  48.3 1.3 %save_results.1 = (bf16[8,32]{1,0:T(8,128)(2,1)}, bf16[8,32]{1,0:T(8,128)(2,1)}, bf16[8,52]{1,0:T(8,128)(2,1)}) custom-call(bf16[8,32]{1,0:T(8,128)(2,1)} %get-tuple-element.9.a, bf16[8,32]{1,0:T(8,128)(2,1)} %get-tuple-element.10.b, bf16[8,52]{1,0:T(8,128)(2,1)} %get-tuple-element.11.c), custom_call_target="tpu_custom_call" | custom-call | tf_op jit(solution)/shard_map/save_results/pallas_call | solution.py:539

commit v5 on v4

--- a/solution.py
+++ b/solution.py
@@ -232,15 +232,6 @@
                 tile = jnp.where(block == yy, moved, tile)
             s1[4 * zq + qq] = encode(tile, lse_tile)
 
-    small[5].wait()
-    small[6].wait()
-    spot = lax.broadcasted_iota(jnp.int32, (32, 128), 1)
-    want = lax.broadcasted_iota(jnp.int32, (32, 128), 0) + 32 * (t % 4)
-    onehot = jnp.where(spot == want, 1.0, 0.0).astype(BF16)
-    rtile = jnp.dot(res_ref[...], onehot, preferred_element_type=F32)
-    rsrc[...] = rtile
-    rbuf[t] = rtile
-    gain32[...] = gain_ref[...].astype(F32).reshape(4, 32, 128)
     zd[3] = s1[z]
     zp[4] = s1[(z + 4) % 16]
     zm[3] = s1[(z + 12) % 16]
@@ -297,6 +288,15 @@
             device_id_type=MESH,
         ).start()
 
+    small[5].wait()
+    small[6].wait()
+    spot = lax.broadcasted_iota(jnp.int32, (32, 128), 1)
+    want = lax.broadcasted_iota(jnp.int32, (32, 128), 0) + 32 * (t % 4)
+    onehot = jnp.where(spot == want, 1.0, 0.0).astype(BF16)
+    rtile = jnp.dot(res_ref[...], onehot, preferred_element_type=F32)
+    rsrc[...] = rtile
+    rbuf[t] = rtile
+    gain32[...] = gain_ref[...].astype(F32).reshape(4, 32, 128)
     pl.semaphore_wait(ready, 1)
     loop(7, send_res)
 

time: 49.7 us -> 49.7 us (level)
  no operation moved by 1% of the time
where the time goes in v5:
time: 49.7 us; the launch traced here: 49.6 us
  Pallas kernels  49 us (99%)
  between operations  0.64 us (1%)
    pallas_call x1, Pallas kernels, body(): pl.pallas_call(kernel, out_shape=(jax.ShapeDtypeStruct((8, 32), BF16), ja...  47.6 us
    pallas_call x1, Pallas kernels, body(): pl.pallas_call(save, out_shape=tuple((jax.ShapeDtypeStruct(a.shape, a.dty...  1.32 us

profile of v5, /device:TPU:1, one launch (start us, length us, event | category | flops | bytes accessed | tf_op | source)
XLA Modules:
  0.0 49.6 jit_solution(5445876455265811416)
XLA Ops:
  0.6 47.6 %decode_layer.1 = (bf16[8,32]{1,0:T(8,128)(2,1)}, bf16[8,32]{1,0:T(8,128)(2,1)}, bf16[8,52]{1,0:T(8,128)(2,1)}) custom-call(s32[8]{0:T(128)} %lengths_ref.1, bf16[8,2048]{1,0:T(8,128)(2,1)} %q_hbm.1, bf16[8,128]{1,0:T(8,128)(2,1)} %ik_hbm.1, bf16[8,128]{1,0:T(8,128)(2,1)} %nv_hbm.1, bf16[512,128]{1,0:T(8,128)(2,1)} %bitcast.6, bf16[512,128]{1,0:T(8,128)(2,1)} %bitcast.7, ...), custom_call_target="tpu_custom_call" | custom-call | tf_op jit(solution)/shard_map/decode_layer/pallas_call | solution.py:477
  48.3 1.3 %save_results.1 = (bf16[8,32]{1,0:T(8,128)(2,1)}, bf16[8,32]{1,0:T(8,128)(2,1)}, bf16[8,52]{1,0:T(8,128)(2,1)}) custom-call(bf16[8,32]{1,0:T(8,128)(2,1)} %get-tuple-element.9.a, bf16[8,32]{1,0:T(8,128)(2,1)} %get-tuple-element.10.b, bf16[8,52]{1,0:T(8,128)(2,1)} %get-tuple-element.11.c), custom_call_target="tpu_custom_call" | custom-call | tf_op jit(solution)/shard_map/save_results/pallas_call | solution.py:539

commit v6 on v4

--- a/solution.py
+++ b/solution.py
@@ -404,6 +404,14 @@
     for g, step in ((3, 0), (2, 3), (1, 1), (0, 2)):
         from_y = (y + 4 - step) % 4
         wait(hbuf.at[pl.ds(0, 8 if step else 7)], h_sems.at[g])
+        if step == 0:
+            source = hbuf[y * 8 + z // 2].astype(F32)
+            half = jnp.where(z % 2 == 0, source[0:8], source[8:16])
+            tile = jnp.where(t // 4 == 0, half[:, 0:128], half[:, 128:256])
+            pick = jnp.where(lane128 == col32 + 32 * (t % 4), 1.0, 0.0).astype(BF16)
+            upd_v[...] = jnp.dot(tile.astype(BF16), pick, preferred_element_type=F32).astype(BF16)
+            upd_save = pltpu.make_async_copy(upd_v, upd_out, local_sems.at[13])
+            upd_save.start()
         gains = gain32[from_y]
         tiles = []
         for m in range(8):
@@ -419,14 +427,6 @@
             part_h, gate_w[:, columns], contract, preferred_element_type=F32
         )
         up = up + lax.dot_general(part_h, up_w[:, columns], contract, preferred_element_type=F32)
-    source = hbuf[y * 8 + z // 2].astype(F32)
-    half = jnp.where(z % 2 == 0, source[0:8], source[8:16])
-    tile = jnp.where(t // 4 == 0, half[:, 0:128], half[:, 128:256])
-    pick = jnp.where(lane128 == col32 + 32 * (t % 4), 1.0, 0.0).astype(BF16)
-    upd_v[...] = jnp.dot(tile.astype(BF16), pick, preferred_element_type=F32).astype(BF16)
-    upd_save = pltpu.make_async_copy(upd_v, upd_out, local_sems.at[13])
-    upd_save.start()
-
     mean = jnp.sum(squares, axis=1, keepdims=True) * (1.0 / 16384)
     inverse = lax.rsqrt(mean + norm_eps)
     gate = gate * inverse

time: 49.7 us -> 49.7 us (level)
  no operation moved by 1% of the time
where the time goes in v6:
time: 49.7 us; the launch traced here: 49.6 us
  Pallas kernels  49 us (99%)
  between operations  0.64 us (1%)
    pallas_call x1, Pallas kernels, body(): pl.pallas_call(kernel, out_shape=(jax.ShapeDtypeStruct((8, 32), BF16), ja...  47.6 us
    pallas_call x1, Pallas kernels, body(): pl.pallas_call(save, out_shape=tuple((jax.ShapeDtypeStruct(a.shape, a.dty...  1.32 us

profile of v6, /device:TPU:1, one launch (start us, length us, event | category | flops | bytes accessed | tf_op | source)
XLA Modules:
  0.0 49.6 jit_solution(1925816425453012654)
XLA Ops:
  0.6 47.6 %decode_layer.1 = (bf16[8,32]{1,0:T(8,128)(2,1)}, bf16[8,32]{1,0:T(8,128)(2,1)}, bf16[8,52]{1,0:T(8,128)(2,1)}) custom-call(s32[8]{0:T(128)} %lengths_ref.1, bf16[8,2048]{1,0:T(8,128)(2,1)} %q_hbm.1, bf16[8,128]{1,0:T(8,128)(2,1)} %ik_hbm.1, bf16[8,128]{1,0:T(8,128)(2,1)} %nv_hbm.1, bf16[512,128]{1,0:T(8,128)(2,1)} %bitcast.6, bf16[512,128]{1,0:T(8,128)(2,1)} %bitcast.7, ...), custom_call_target="tpu_custom_call" | custom-call | tf_op jit(solution)/shard_map/decode_layer/pallas_call | solution.py:477
  48.3 1.3 %save_results.1 = (bf16[8,32]{1,0:T(8,128)(2,1)}, bf16[8,32]{1,0:T(8,128)(2,1)}, bf16[8,52]{1,0:T(8,128)(2,1)}) custom-call(bf16[8,32]{1,0:T(8,128)(2,1)} %get-tuple-element.9.a, bf16[8,32]{1,0:T(8,128)(2,1)} %get-tuple-element.10.b, bf16[8,52]{1,0:T(8,128)(2,1)} %get-tuple-element.11.c), custom_call_target="tpu_custom_call" | custom-call | tf_op jit(solution)/shard_map/save_results/pallas_call | solution.py:539
